TPU v7x, 32 devices: a whole 2x2x4 slice. The times are simulated.
32 devices in a mesh: tm: 2 (over x), tensor: 4 (over y, core), dp: 4 (over z).
Axes of the slice: x: 2, y: 2, z: 4, core: 2. Of those that a mesh axis runs over, the one named last changes fastest.
Arguments:
- video: bfloat16 [4, 2, 256, 1280], P('dp', 'tm'), may hold values from -6 to 6
- w_spatial: bfloat16 [3, 1280, 1280], P(None, 'dp', 'tensor'), as said below
- w_spatial_out: bfloat16 [1280, 1280], P('tensor', 'dp'), may hold values from -0.15625 to 0.15625
- temporal_weight: bfloat16 [3, 1280, 1280], P(None, 'dp', 'tensor'), as said below
- temporal_output_weight: bfloat16 [1280, 1280], P('tensor', 'dp'), may hold values from -0.15625 to 0.15625
- merger: bfloat16 [4, 1280, 8192], P(None, 'tensor', 'tm'), may hold values from -0.078125 to 0.078125
- text: bfloat16 [512, 8192], P('dp', 'tm'), may hold values from -6 to 6
- norm_gain: float32 [8192], P('tm'), may hold values from 0.1 to 1.9
- w_gate: bfloat16 [8192, 15360], P('tm', ('tensor', 'dp')), may hold values from -0.0625 to 0.0625
- w_up: bfloat16 [8192, 15360], P('tm', ('tensor', 'dp')), may hold values from -0.0625 to 0.0625
- w_down: bfloat16 [15360, 8192], P(('tensor', 'dp'), 'tm'), may hold values from -0.046875 to 0.046875
- probe: bfloat16 [512, 8192], P(None, 'tm'), may hold values from -0.25 to 0.25
- ref_margin: float32 [16], replicated, may hold values from -0.5 to 0.5
- pair_ids: int32 [512], replicated, may hold values from 0 to 3
- labels: int32 [512], replicated, may hold values from -1 to 1
- positions: int32 [512], P('dp'), may hold values from 0 to 127
Outputs:
- losses: float32 [16], replicated
- grad_gate: bfloat16 [8192, 15360], P('tm', ('tensor', 'dp'))
- grad_up: bfloat16 [8192, 15360], P('tm', ('tensor', 'dp'))
- grad_down: bfloat16 [15360, 8192], P(('tensor', 'dp'), 'tm')
Inputs may be any that keep to these rules, and one draw needn't show every extreme that they name: `w_spatial`: queries, keys and values in this order along the first dimension. `temporal_weight`: queries, keys and values in this order along the first dimension. `labels`: 1 for a chosen rollout's row, -1 for a rejected one's, 0 for a row outside the loss. `positions`: index f * 64 + g of the merged token, frame f and group g of four consecutive patches.
All inputs are finite; a program needn't handle non-finite values.
Results may differ from a plain program's by a relative error of at most 0.035.
Values may be sent and summed in bfloat16 or wider, within the bound.
A program may use at most 128 MiB of HBM per device.

v0:
```python
import jax
import jax.numpy as jnp
from jax import lax
from jax.sharding import PartitionSpec as P

W = 1280
HEADS = 16
D = 8192
ROWS = 128
PAIRS_DEV = 4


beta_scale = 0.1
loss_scale = 256.0
norm_eps = 1e-06


def layer_norm(values):
    centered = values - jnp.mean(values, axis=-1, keepdims=True)
    spread = jnp.mean(centered * centered, axis=-1, keepdims=True)
    return centered * lax.rsqrt(spread + norm_eps)


def attend(queries, key_rows, value_rows, head_size):
    leading = queries.shape[:-1]
    head_count = queries.shape[-1] // head_size

    def head_split(tensor_in):
        return tensor_in.reshape(tensor_in.shape[:-1] + (head_count, head_size))

    scores = jnp.einsum(
        "...qhd,...khd->...hqk",
        head_split(queries),
        head_split(key_rows),
        preferred_element_type=jnp.float32,
    ) * head_size ** (-0.5)
    weights_soft = jax.nn.softmax(scores, axis=-1).astype(jnp.bfloat16)
    attended_context = jnp.einsum(
        "...hqk,...khd->...qhd",
        weights_soft,
        head_split(value_rows),
        preferred_element_type=jnp.float32,
    )
    return attended_context.astype(jnp.bfloat16).reshape(leading + (head_count * head_size,))


def body(
    video,
    w_spatial,
    w_spatial_out,
    temporal_weight,
    temporal_output_weight,
    merger,
    text,
    norm_gain,
    w_gate,
    w_up,
    w_down,
    probe,
    ref_margin,
    pair_ids,
    labels,
    positions,
):
    head_size = W // HEADS
    tensor_count = lax.axis_size("tensor")
    tensor_index = lax.axis_index("tensor")
    tm_index = lax.axis_index("tm")
    spatial_w, spatial_out, temporal_w, temporal_output = (
        lax.all_gather(w_spatial, "dp", axis=1, tiled=True),
        lax.all_gather(w_spatial_out, "dp", axis=1, tiled=True),
        lax.all_gather(temporal_weight, "dp", axis=1, tiled=True),
        lax.all_gather(temporal_output_weight, "dp", axis=1, tiled=True),
    )
    frames = video[0]
    patches = frames.shape[1]
    width = frames.shape[2]

    def spatial_frame(one_frame):
        normed_input = layer_norm(one_frame.astype(jnp.float32)).astype(jnp.bfloat16)
        project = jnp.einsum(
            "pw,jwc->jpc", normed_input, spatial_w, preferred_element_type=jnp.float32
        ).astype(jnp.bfloat16)
        attended_context = attend(project[0], project[1], project[2], head_size)
        return jnp.dot(attended_context, spatial_out, preferred_element_type=jnp.float32)

    partial_out = lax.map(spatial_frame, frames)
    summed = lax.psum(partial_out.astype(jnp.bfloat16), "tensor").astype(jnp.float32)
    mixed = (frames.astype(jnp.float32) + summed).astype(jnp.bfloat16)
    arrived = lax.all_to_all(mixed, "tm", split_axis=1, concat_axis=0, tiled=True)
    frame_count = arrived.shape[0]
    normed_t = layer_norm(arrived.astype(jnp.float32)).astype(jnp.bfloat16)
    project_t = jnp.einsum(
        "fpw,jwc->jpfc", normed_t, temporal_w, preferred_element_type=jnp.float32
    ).astype(jnp.bfloat16)
    temporal_context = attend(project_t[0], project_t[1], project_t[2], head_size)
    partial_t = jnp.einsum(
        "lby,yd->bld", temporal_context, temporal_output, preferred_element_type=jnp.float32
    )
    temporal_sum = lax.psum_scatter(
        partial_t.astype(jnp.bfloat16), "tensor", scatter_dimension=2, tiled=True
    ).astype(jnp.float32)
    quarter = width // tensor_count
    residual_cols = lax.dynamic_slice_in_dim(arrived, tensor_index * quarter, quarter, 2)
    encoded = (residual_cols.astype(jnp.float32) + temporal_sum).astype(jnp.bfloat16)
    groups_local = encoded.shape[1] // 4
    merged = encoded.reshape(frame_count * groups_local, 4 * quarter)
    groups_frame = patches // 4
    frame_of = positions // groups_frame
    group_of = positions % groups_frame
    owner_tm = group_of // groups_local
    slot_group = group_of % groups_local
    slot_index = frame_of * groups_local + slot_group
    hit_table = (
        slot_index[:, None] == jnp.arange(frame_count * groups_local, dtype=jnp.int32)[None, :]
    ) & (owner_tm == tm_index)[:, None]
    picked = jnp.dot(hit_table.astype(jnp.bfloat16), merged, preferred_element_type=jnp.float32)
    chosen_tokens = lax.psum(picked.astype(jnp.bfloat16), "tm")
    vis_part = jnp.dot(
        chosen_tokens,
        merger.reshape(4 * quarter, merger.shape[2]),
        preferred_element_type=jnp.float32,
    )
    visual = lax.psum(vis_part.astype(jnp.bfloat16), "tensor").astype(jnp.float32)
    hidden_in = text.astype(jnp.float32) + visual
    square_sum = lax.psum(jnp.sum(hidden_in * hidden_in, axis=1), "tm")
    normed_rows = (
        hidden_in * lax.rsqrt(square_sum / D + norm_eps)[:, None] * norm_gain[None, :]
    ).astype(jnp.bfloat16)
    all_rows = lax.all_gather(normed_rows, "dp", axis=0, tiled=True)
    total_rows = all_rows.shape[0]
    hidden_cols = w_gate.shape[1]
    row_block = all_rows
    gate_up = lax.psum_scatter(
        jnp.concatenate(
            [
                jnp.dot(row_block, w_gate, preferred_element_type=jnp.float32),
                jnp.dot(row_block, w_up, preferred_element_type=jnp.float32),
            ],
            axis=1,
        ).astype(jnp.bfloat16),
        "tm",
        scatter_dimension=0,
        tiled=True,
    ).astype(jnp.float32)
    gate_pre = gate_up[:, :hidden_cols]
    up_pre = gate_up[:, hidden_cols:]
    sig_gate = jax.nn.sigmoid(gate_pre)
    hidden_local = (gate_pre * sig_gate * up_pre).astype(jnp.bfloat16)
    hidden_all = lax.all_gather(hidden_local, "tm", axis=0, tiled=True)
    pair_total = ref_margin.shape[0]
    delta_part = jnp.dot(hidden_all, w_down, preferred_element_type=jnp.float32)
    probe_wide = probe.astype(jnp.float32)
    row_index = jnp.arange(total_rows, dtype=jnp.int32)
    global_pair = row_index // ROWS * PAIRS_DEV + pair_ids[row_index]
    member = (global_pair[:, None] == jnp.arange(pair_total, dtype=jnp.int32)[None, :]).astype(
        jnp.float32
    )
    signed = labels[row_index].astype(jnp.float32)
    margin = lax.psum(
        jnp.dot(
            signed * jnp.sum(delta_part * probe_wide, axis=1),
            member,
            precision=lax.Precision.HIGHEST,
        ),
        ("tm", "tensor", "dp"),
    )
    logits = beta_scale * margin - ref_margin
    losses = jax.nn.softplus(-logits)
    coefficient = -beta_scale * loss_scale * jax.nn.sigmoid(-logits)
    row_coef = jnp.dot(member, coefficient, precision=lax.Precision.HIGHEST) * signed
    losses, row_coef = (losses, row_coef)
    cotangent = (row_coef[:, None] * probe_wide).astype(jnp.bfloat16)
    grad_down = lax.dot_general(
        hidden_all, cotangent, (((0,), (0,)), ((), ())), preferred_element_type=jnp.float32
    ).astype(jnp.bfloat16)
    row_block = cotangent
    hidden_grad = lax.psum_scatter(
        lax.dot_general(
            row_block, w_down, (((1,), (1,)), ((), ())), preferred_element_type=jnp.float32
        ).astype(jnp.bfloat16),
        "tm",
        scatter_dimension=0,
        tiled=True,
    ).astype(jnp.float32)
    gate_grad = (hidden_grad * up_pre * sig_gate * (1.0 + gate_pre * (1.0 - sig_gate))).astype(
        jnp.bfloat16
    )
    up_grad = (hidden_grad * gate_pre * sig_gate).astype(jnp.bfloat16)
    row_block = all_rows
    gate_term = lax.dot_general(
        row_block,
        lax.all_gather(gate_grad, "tm", axis=0, tiled=True),
        (((0,), (0,)), ((), ())),
        preferred_element_type=jnp.float32,
    )
    up_term = lax.dot_general(
        row_block,
        lax.all_gather(up_grad, "tm", axis=0, tiled=True),
        (((0,), (0,)), ((), ())),
        preferred_element_type=jnp.float32,
    )
    return (losses, gate_term.astype(jnp.bfloat16), up_term.astype(jnp.bfloat16), grad_down)


def solution(mesh):
    return jax.shard_map(
        body,
        mesh=mesh,
        in_specs=(
            P("dp", "tm", None, None),
            P(None, "dp", "tensor"),
            P("tensor", "dp"),
            P(None, "dp", "tensor"),
            P("tensor", "dp"),
            P(None, "tensor", "tm"),
            P("dp", "tm"),
            P("tm"),
            P("tm", ("tensor", "dp")),
            P("tm", ("tensor", "dp")),
            P(("tensor", "dp"), "tm"),
            P(None, "tm"),
            P(),
            P(),
            P(),
            P("dp"),
        ),
        out_specs=(
            P(),
            P("tm", ("tensor", "dp")),
            P("tm", ("tensor", "dp")),
            P(("tensor", "dp"), "tm"),
        ),
        check_vma=False,
    )
```

profile of v0, /device:TPU:0, one launch (start us, length us, event | category | flops | bytes accessed | tf_op | source)
XLA Modules:
  0.0 642.6 jit_solution(16491784604029433321)
XLA Ops:
  12.8 35.1 %all_gather.25 = bf16[320,1280]{0,1:T(8,128)(2,1)S(1)} all-gather(bf16[320,320]{0,1:T(8,128)(2,1)S(1)} %copy.55), channel_id=1, replica_groups=mesh['tm'=2,'tensor'=4,'dp'=4] {'dp'}, dimensions={1}, use_global_device_ids=true | all-gather | bytes 1024000 | tf_op jit(solution)/shard_map/all_gather | solution.py:71
  47.9 51.2 %all-gather.4.cloned.1.call-done = bf16[3,1280,320]{2,0,1:T(4,128)(2,1)} async-done(((bf16[3,320,320]{2,0,1:T(4,128)(2,1)}), bf16[3,1280,320]{2,0,1:T(4,128)(2,1)}) %all-gather.4.cloned.1.call-update) | async-done | bytes 2457616 | tf_op jit(solution)/shard_map/all_gather | solution.py:70
  111.9 32.0 %all-reduce.6.cloned.1.call-done = bf16[1,256,1280]{2,1,0:T(8,128)(2,1)} async-done(((bf16[1,256,1280]{2,1,0:T(8,128)(2,1)}), bf16[1,256,1280]{2,1,0:T(8,128)(2,1)}) %all-reduce.6.cloned.1.call-update) | async-done | bytes 655376 | tf_op jit(solution)/shard_map/psum | solution.py:88
  156.2 36.1 %all_gather.27 = bf16[320,1280]{0,1:T(8,128)(2,1)S(1)} all-gather(bf16[320,320]{0,1:T(8,128)(2,1)S(1)} %copy.64), channel_id=1, replica_groups=mesh['tm'=2,'tensor'=4,'dp'=4] {'dp'}, dimensions={1}, use_global_device_ids=true | all-gather | bytes 1024000 | tf_op jit(solution)/shard_map/all_gather | solution.py:73
  192.3 45.8 %all-gather.6.cloned.1.call-done = bf16[3,1280,320]{2,0,1:T(4,128)(2,1)} async-done(((bf16[3,320,320]{2,0,1:T(4,128)(2,1)}), bf16[3,1280,320]{2,0,1:T(4,128)(2,1)}) %all-gather.6.cloned.1.call-update) | async-done | bytes 2457616 | tf_op jit(solution)/shard_map/all_gather | solution.py:72
  238.1 7.4 %copy.58 = bf16[3,1280,320]{1,2,0:T(8,128)(2,1)} copy(bf16[3,1280,320]{2,0,1:T(4,128)(2,1)} %all-gather.6.cloned.1.call-done) | data formatting | bytes 4915200 | tf_op jit(solution)/shard_map/all_gather | solution.py:72
  262.2 31.1 %all-reduce.12.cloned.1.call-done = bf16[2,128,1280]{1,0,2:T(2,128)(2,1)} async-done(((bf16[2,128,1280]{1,0,2:T(2,128)(2,1)}), bf16[2,128,1280]{1,0,2:T(2,128)(2,1)}) %all-reduce.12.cloned.1.call-update) | async-done | bytes 655376
  296.2 24.2 %all-reduce.8.cloned.1.call-done = bf16[128,1280]{1,0:T(8,128)(2,1)} async-done(((bf16[128,1280]{1,0:T(8,128)(2,1)}), bf16[128,1280]{1,0:T(8,128)(2,1)}) %all-reduce.8.cloned.1.call-update) | async-done | bytes 327696 | tf_op jit(solution)/shard_map/psum | solution.py:118
  320.4 6.7 %convolution_convert_fusion.3 = bf16[128,4096]{1,0:T(8,128)(2,1)} fusion(bf16[128,1280]{1,0:T(8,128)(2,1)} %all-reduce.8.cloned.1.call-done, bf16[1280,4096]{1,0:T(8,128)(2,1)} %bitcast.113), kind=kOutput, calls=%fused_computation.11 | convolution fusion | flops 1342701568 | bytes 11862016 | tf_op jit(solution)/shard_map/dot_general | solution.py:119
  327.1 36.2 %all-reduce.10.cloned.1.call-done = bf16[128,4096]{1,0:T(8,128)(2,1)} async-done(((bf16[128,4096]{1,0:T(8,128)(2,1)}), bf16[128,4096]{1,0:T(8,128)(2,1)}) %all-reduce.10.cloned.1.call-update) | async-done | bytes 1048592 | tf_op jit(solution)/shard_map/psum | solution.py:124
  372.7 81.2 %all-gather.8.cloned.1.call-done = bf16[512,4096]{1,0:T(8,128)(2,1)} async-done(((bf16[128,4096]{1,0:T(8,128)(2,1)}), bf16[512,4096]{1,0:T(8,128)(2,1)}) %all-gather.8.cloned.1.call-update) | async-done | bytes 4194320 | tf_op jit(solution)/shard_map/all_gather | solution.py:130
  454.0 8.9 %convolution_convert_fusion.7 = bf16[512,960]{0,1:T(8,128)(2,1)S(1)} fusion(bf16[512,4096]{1,0:T(8,128)(2,1)} %all-gather.8.cloned.1.call-done, bf16[4096,960]{0,1:T(8,128)(2,1)} %param.25), kind=kOutput, calls=%fused_computation.31 | convolution fusion | flops 4027023360 | bytes 13041664 | tf_op jit(solution)/shard_map/dot_general | solution.py:138
  462.9 6.8 %convolution_convert_fusion.8 = bf16[512,960]{0,1:T(8,128)(2,1)S(1)} fusion(bf16[512,4096]{1,0:T(8,128)(2,1)S(1)} %copy-done.13, bf16[4096,960]{0,1:T(8,128)(2,1)} %param.24), kind=kOutput, calls=%fused_computation.32 | convolution fusion | flops 4027023360 | bytes 13041664 | tf_op jit(solution)/shard_map/dot_general | solution.py:137
  478.2 21.9 %reduce-scatter.3.cloned.1.call-done = bf16[256,1920]{0,1:T(8,128)(2,1)} async-done(((bf16[512,1920]{0,1:T(8,128)(2,1)}), bf16[256,1920]{0,1:T(8,128)(2,1)}) %reduce-scatter.3.cloned.1.call-update) | async-done | bytes 983056 | tf_op jit(solution)/shard_map/reduce_scatter | solution.py:134
  502.0 13.9 %all_gather.29 = bf16[512,960]{0,1:T(8,128)(2,1)S(1)} all-gather(bf16[256,960]{0,1:T(8,128)(2,1)S(1)} %multiply_convert_fusion.2), channel_id=1, replica_groups=mesh['tm'=2,'tensor'=4,'dp'=4] {'tm'}, dimensions={0}, use_global_device_ids=true | all-gather | bytes 1474560 | tf_op jit(solution)/shard_map/all_gather | solution.py:150
  515.9 8.4 %fusion.2 = f32[512]{0:T(512)S(1)} fusion(bf16[512,4096]{1,0:T(8,128)(2,1)S(1)} %copy-done.12, bf16[512,960]{0,1:T(8,128)(2,1)S(1)} %all_gather.29, bf16[960,4096]{1,0:T(8,128)(2,1)} %param.26), kind=kOutput, calls=%fused_computation.6 | convolution fusion | flops 4032822784 | bytes 13043712 | tf_op jit(solution)/shard_map/dot_general | solution.py:152
  524.5 39.4 %psum.39 = f32[16]{0:T(128)S(1)} all-reduce(f32[16]{0:T(128)S(1)} %convolution_bitcast_fusion), channel_id=1, replica_groups=mesh['tm'=2,'tensor'=4,'dp'=4] {'tm','tensor','dp'}, use_global_device_ids=true, to_apply=%region_16.17 | all-reduce | flops 16 | bytes 128 | tf_op jit(solution)/shard_map/psum | solution.py:160
  564.2 9.8 %fusion.14 = bf16[512,960]{0,1:T(8,128)(2,1)} fusion(bf16[960,4096]{1,0:T(8,128)(2,1)} %param.26, bf16[512,4096]{1,0:T(8,128)(2,1)} %param.27, f32[512]{0:T(512)S(1)} %convert_multiply_fusion.4), kind=kOutput, calls=%fused_computation.30 | convolution fusion | flops 4033314816 | bytes 13043712 | tf_op jit(solution)/shard_map/dot_general | solution.py:179
  574.6 8.9 %convolution_convert_fusion.2 = bf16[960,4096]{1,0:T(8,128)(2,1)} fusion(bf16[512,960]{0,1:T(8,128)(2,1)S(1)} %all_gather.29, bf16[512,4096]{1,0:T(8,128)(2,1)} %param.27, f32[512]{0:T(512)S(1)} %convert_multiply_fusion.4), kind=kOutput, calls=%fused_computation.10 | convolution fusion | flops 4036755456 | bytes 13043712 | tf_op jit(solution)/shard_map/dot_general | solution.py:174
  583.5 11.0 %reduce-scatter.5.cloned.1.call-done = bf16[256,960]{0,1:T(8,128)(2,1)} async-done(((bf16[512,960]{0,1:T(8,128)(2,1)}), bf16[256,960]{0,1:T(8,128)(2,1)}) %reduce-scatter.5.cloned.1.call-update) | async-done | bytes 491536 | tf_op jit(solution)/shard_map/reduce_scatter | solution.py:178
  596.2 13.6 %all_gather.30 = bf16[512,960]{0,1:T(8,128)(2,1)S(1)} all-gather(bf16[256,960]{0,1:T(8,128)(2,1)S(1)} %get-tuple-element.23), channel_id=1, replica_groups=mesh['tm'=2,'tensor'=4,'dp'=4] {'tm'}, dimensions={0}, use_global_device_ids=true | all-gather | bytes 1474560 | tf_op jit(solution)/shard_map/all_gather | solution.py:193
  609.8 13.0 %all_gather.31 = bf16[512,960]{0,1:T(8,128)(2,1)S(1)} all-gather(bf16[256,960]{0,1:T(8,128)(2,1)S(1)} %get-tuple-element.22), channel_id=1, replica_groups=mesh['tm'=2,'tensor'=4,'dp'=4] {'tm'}, dimensions={0}, use_global_device_ids=true | all-gather | bytes 1474560 | tf_op jit(solution)/shard_map/all_gather | solution.py:199
  622.9 6.3 convolution_convert_fusion.1
  629.2 6.3 convolution_convert_fusion
  (116 shorter events, 71.8 us)
Async XLA Ops:
  7.2 464.0 %copy-start = (s32[512]{0:T(512)S(1)}, s32[512]{0:T(512)}, u32[]{:S(2)}) copy-start(s32[512]{0:T(512)} %param.30) | copy-start | bytes 6148
  7.2 5.3 copy-start.3
  7.2 91.9 %all-gather.4.cloned.1.call-start = ((), (), s32[]{:S(2)}) async-start(), calls=%async_computation.3 | async-start | bytes 4915200 | tf_op jit(solution)/shard_map/all_gather | solution.py:70
  10.0 133.8 %all-reduce.6.cloned.1.call-start = ((), (), s32[]{:S(2)}) async-start(), calls=%async_computation.4 | async-start | bytes 1310720 | tf_op jit(solution)/shard_map/psum | solution.py:88
  104.5 5.8 copy-start.6
  110.2 127.9 %all-gather.6.cloned.1.call-start = ((), (), s32[]{:S(2)}) async-start(), calls=%async_computation.5 | async-start | bytes 4915200 | tf_op jit(solution)/shard_map/all_gather | solution.py:72
  111.8 44.1 %copy-start.9 = (bf16[320,320]{1,0:T(8,128)(2,1)S(1)}, bf16[320,320]{1,0:T(8,128)(2,1)}, u32[]{:S(2)}) copy-start(bf16[320,320]{1,0:T(8,128)(2,1)} %param.20) | copy-start | bytes 614404
  152.4 93.2 %all-to-all-start = ((bf16[2,2,81920]{2,1,0:T(2,128)(2,1)}), bf16[2,2,81920]{2,1,0:T(2,128)(2,1)S(1)}, u32[]{:S(2)}, u32[]{:S(2)}) async-start(bf16[2,2,81920]{2,1,0:T(2,128)(2,1)} %reshape.145), calls=%async_computation | async-start | bytes 1310720 | tf_op jit(solution)/shard_map/all_to_all | solution.py:90
  155.9 137.4 %all-reduce.12.cloned.1.call-start = ((), (), s32[]{:S(2)}) async-start(), calls=%async_computation.11 | async-start | bytes 1310720
  246.1 5.3 copy-start.5
  258.2 2.7 copy-start.16
  260.8 59.6 %all-reduce.8.cloned.1.call-start = ((), (), s32[]{:S(2)}) async-start(), calls=%async_computation.6 | async-start | bytes 655360 | tf_op jit(solution)/shard_map/psum | solution.py:118
  295.9 67.4 %all-reduce.10.cloned.1.call-start = ((), (), s32[]{:S(2)}) async-start(), calls=%async_computation.7 | async-start | bytes 2097152 | tf_op jit(solution)/shard_map/psum | solution.py:124
  320.4 43.0 %copy-start.4 = (bf16[128,4096]{1,0:T(8,128)(2,1)S(1)}, bf16[128,4096]{1,0:T(8,128)(2,1)}, u32[]{:S(2)}) copy-start(bf16[128,4096]{1,0:T(8,128)(2,1)} %param.22) | copy-start | bytes 3145732
  320.4 49.6 %copy-start.10 = (f32[4096]{0:T(1024)S(1)}, f32[4096]{0:T(1024)}, u32[]{:S(2)}) copy-start(f32[4096]{0:T(1024)} %param.23) | copy-start | bytes 49156
  327.1 126.9 %all-gather.8.cloned.1.call-start = ((), (), s32[]{:S(2)}) async-start(), calls=%async_computation.8 | async-start | bytes 5242880 | tf_op jit(solution)/shard_map/all_gather | solution.py:130
  372.7 127.5 %reduce-scatter.3.cloned.1.call-start = ((), (), s32[]{:S(2)}) async-start(), calls=%async_computation.9 | async-start | bytes 2949120 | tf_op jit(solution)/shard_map/reduce_scatter | solution.py:134
  454.0 8.9 %copy-start.13 = (bf16[512,4096]{1,0:T(8,128)(2,1)S(1)}, bf16[512,4096]{1,0:T(8,128)(2,1)}, u32[]{:S(2)}) copy-start(bf16[512,4096]{1,0:T(8,128)(2,1)} %all-gather.8.cloned.1.call-done) | copy-start | bytes 12582916
  469.6 5.0 copy-start.2
  471.1 123.4 %reduce-scatter.5.cloned.1.call-start = ((), (), s32[]{:S(2)}) async-start(), calls=%async_computation.10 | async-start | bytes 1474560 | tf_op jit(solution)/shard_map/reduce_scatter | solution.py:178
  500.1 15.7 %copy-start.12 = (bf16[512,4096]{1,0:T(8,128)(2,1)S(1)}, bf16[512,4096]{1,0:T(8,128)(2,1)}, u32[]{:S(2)}) copy-start(bf16[512,4096]{1,0:T(8,128)(2,1)} %param.27) | copy-start | bytes 12582916
  515.9 48.0 %copy-start.15 = (f32[16]{0:T(128)S(1)}, f32[16]{0:T(128)}, u32[]{:S(2)}) copy-start(f32[16]{0:T(128)} %param.28) | copy-start | bytes 196
  594.5 28.3 %copy-start.14 = (bf16[512,4096]{1,0:T(8,128)(2,1)S(1)}, bf16[512,4096]{1,0:T(8,128)(2,1)}, u32[]{:S(2)}) copy-start(bf16[512,4096]{1,0:T(8,128)(2,1)} %all-gather.8.cloned.1.call-done) | copy-start | bytes 12582916
  629.2 6.4 copy-start.1
  (3 other events, 4.0 us)
Sparse Core Ops, SparseCore 0:
  10.2 88.8 all-gather.3
  110.3 33.4 all-reduce.5
  146.0 92.0 all-gather.5
  260.9 32.3 all-reduce.11
  296.0 24.2 all-reduce.7
  327.2 36.1 all-reduce.9
  372.8 81.1 all-gather.7
  471.2 28.8 reduce-scatter.2
  574.2 20.3 reduce-scatter.4
where the time goes:
time: 651 us; the launch traced here: 643 us
  waiting for transfers between devices  335 us (51%)
  blocking collectives  156 us (24%)
  matrix products  80 us (12%)
  local copies, waits for them, and re-layouts  29.4 us (5%)
  other arithmetic  22.8 us (4%)
  between operations  15.4 us (2%)
    all_gather x1, waiting for transfers between devices, body(): all_rows = lax.all_gather(normed_rows, 'dp', axis=0, tiled=True)  81.2 us
    all_gather x1, waiting for transfers between devices, body(): lax.all_gather(w_spatial, 'dp', axis=1, tiled=True)  51.2 us
    all_gather x1, waiting for transfers between devices, body(): lax.all_gather(temporal_weight, 'dp', axis=1, tiled=True)  45.8 us
    psum x1, blocking collectives, body(): lax.psum(jnp.dot(signed * jnp.sum(delta_part * probe_wide, axis=1), membe...  39.4 us
    psum x1, waiting for transfers between devices, body(): lax.psum(vis_part.astype(jnp.bfloat16), 'tensor').astype(jnp.float32)  36.2 us
    all_gather x1, blocking collectives, body(): lax.all_gather(temporal_output_weight, 'dp', axis=1, tiled=True)  36.1 us
    all_gather x1, blocking collectives, body(): lax.all_gather(w_spatial_out, 'dp', axis=1, tiled=True)  35.1 us
    psum x1, waiting for transfers between devices, body(): lax.psum(partial_out.astype(jnp.bfloat16), 'tensor').astype(jnp.float32)  32 us
  transfers between devices with their start and end apart: 10, of which 9 were waited for; matrix products, arithmetic and copies ran while one was open for 6% of the time, Pallas kernels for 0%

commit v1 on v0

--- a/solution.py
+++ b/solution.py
@@ -66,12 +66,26 @@
     tensor_count = lax.axis_size("tensor")
     tensor_index = lax.axis_index("tensor")
     tm_index = lax.axis_index("tm")
-    spatial_w, spatial_out, temporal_w, temporal_output = (
-        lax.all_gather(w_spatial, "dp", axis=1, tiled=True),
-        lax.all_gather(w_spatial_out, "dp", axis=1, tiled=True),
-        lax.all_gather(temporal_weight, "dp", axis=1, tiled=True),
-        lax.all_gather(temporal_output_weight, "dp", axis=1, tiled=True),
-    )
+    total_rows = probe.shape[0]
+    probe_part = lax.dot_general(
+        probe, w_down, (((1,), (1,)), ((), ())), preferred_element_type=jnp.float32
+    ).astype(jnp.bfloat16)
+
+    def gathered(qkv, out):
+        whole = lax.all_gather(jnp.concatenate([qkv, out[None]], axis=0), "dp", axis=0)
+        n, _, rows, cols = whole.shape
+        return (
+            whole[:, :3].transpose(1, 0, 2, 3).reshape(3, n * rows, cols),
+            whole[:, 3].transpose(1, 0, 2).reshape(rows, n * cols),
+        )
+
+    spatial_w, spatial_out = gathered(w_spatial, w_spatial_out)
+    temporal_weight, temporal_output_weight, spatial_w, probe_part = lax.optimization_barrier(
+        (temporal_weight, temporal_output_weight, spatial_w, probe_part)
+    )
+    temporal_w, temporal_output = gathered(temporal_weight, temporal_output_weight)
+    probe_down = lax.psum_scatter(probe_part, "tm", scatter_dimension=0, tiled=True)
+    temporal_w, probe_down = lax.optimization_barrier((temporal_w, probe_down))
     frames = video[0]
     patches = frames.shape[1]
     width = frames.shape[2]
@@ -121,14 +135,17 @@
         merger.reshape(4 * quarter, merger.shape[2]),
         preferred_element_type=jnp.float32,
     )
-    visual = lax.psum(vis_part.astype(jnp.bfloat16), "tensor").astype(jnp.float32)
-    hidden_in = text.astype(jnp.float32) + visual
+    visual = lax.psum_scatter(
+        vis_part.astype(jnp.bfloat16), "tensor", scatter_dimension=0, tiled=True
+    ).astype(jnp.float32)
+    own_rows = visual.shape[0]
+    text_own = lax.dynamic_slice_in_dim(text, tensor_index * own_rows, own_rows, 0)
+    hidden_in = text_own.astype(jnp.float32) + visual
     square_sum = lax.psum(jnp.sum(hidden_in * hidden_in, axis=1), "tm")
     normed_rows = (
         hidden_in * lax.rsqrt(square_sum / D + norm_eps)[:, None] * norm_gain[None, :]
     ).astype(jnp.bfloat16)
-    all_rows = lax.all_gather(normed_rows, "dp", axis=0, tiled=True)
-    total_rows = all_rows.shape[0]
+    all_rows = lax.all_gather(normed_rows, ("dp", "tensor"), axis=0, tiled=True)
     hidden_cols = w_gate.shape[1]
     row_block = all_rows
     gate_up = lax.psum_scatter(
@@ -147,60 +164,49 @@
     up_pre = gate_up[:, hidden_cols:]
     sig_gate = jax.nn.sigmoid(gate_pre)
     hidden_local = (gate_pre * sig_gate * up_pre).astype(jnp.bfloat16)
-    hidden_all = lax.all_gather(hidden_local, "tm", axis=0, tiled=True)
+    probe_grad = probe_down.astype(jnp.float32)
+    gate_slope = (probe_grad * up_pre * sig_gate * (1.0 + gate_pre * (1.0 - sig_gate))).astype(
+        jnp.bfloat16
+    )
+    up_slope = (probe_grad * gate_pre * sig_gate).astype(jnp.bfloat16)
     pair_total = ref_margin.shape[0]
-    delta_part = jnp.dot(hidden_all, w_down, preferred_element_type=jnp.float32)
-    probe_wide = probe.astype(jnp.float32)
     row_index = jnp.arange(total_rows, dtype=jnp.int32)
-    global_pair = row_index // ROWS * PAIRS_DEV + pair_ids[row_index]
+    global_pair = row_index // ROWS * PAIRS_DEV + pair_ids
     member = (global_pair[:, None] == jnp.arange(pair_total, dtype=jnp.int32)[None, :]).astype(
         jnp.float32
     )
-    signed = labels[row_index].astype(jnp.float32)
-    margin = lax.psum(
-        jnp.dot(
-            signed * jnp.sum(delta_part * probe_wide, axis=1),
-            member,
-            precision=lax.Precision.HIGHEST,
-        ),
-        ("tm", "tensor", "dp"),
-    )
+    signed = labels.astype(jnp.float32)
+    local_rows = hidden_local.shape[0]
+    score = jnp.sum(hidden_local.astype(jnp.float32) * probe_grad, axis=1)
+    margin = jnp.dot(
+        lax.dynamic_slice_in_dim(signed, tm_index * local_rows, local_rows, 0) * score,
+        lax.dynamic_slice_in_dim(member, tm_index * local_rows, local_rows, 0),
+        precision=lax.Precision.HIGHEST,
+    )
+    for axis in ("tensor", "dp", "tm"):
+        margin = lax.optimization_barrier(lax.psum(margin, axis))
+    shared = lax.all_gather(
+        jnp.concatenate([hidden_local, gate_slope, up_slope], axis=1), "tm", axis=0, tiled=True
+    )
+    hidden_all = shared[:, :hidden_cols]
     logits = beta_scale * margin - ref_margin
     losses = jax.nn.softplus(-logits)
     coefficient = -beta_scale * loss_scale * jax.nn.sigmoid(-logits)
     row_coef = jnp.dot(member, coefficient, precision=lax.Precision.HIGHEST) * signed
-    losses, row_coef = (losses, row_coef)
-    cotangent = (row_coef[:, None] * probe_wide).astype(jnp.bfloat16)
-    grad_down = lax.dot_general(
-        hidden_all, cotangent, (((0,), (0,)), ((), ())), preferred_element_type=jnp.float32
-    ).astype(jnp.bfloat16)
-    row_block = cotangent
-    hidden_grad = lax.psum_scatter(
-        lax.dot_general(
-            row_block, w_down, (((1,), (1,)), ((), ())), preferred_element_type=jnp.float32
-        ).astype(jnp.bfloat16),
-        "tm",
-        scatter_dimension=0,
-        tiled=True,
-    ).astype(jnp.float32)
-    gate_grad = (hidden_grad * up_pre * sig_gate * (1.0 + gate_pre * (1.0 - sig_gate))).astype(
-        jnp.bfloat16
-    )
-    up_grad = (hidden_grad * gate_pre * sig_gate).astype(jnp.bfloat16)
-    row_block = all_rows
-    gate_term = lax.dot_general(
-        row_block,
-        lax.all_gather(gate_grad, "tm", axis=0, tiled=True),
-        (((0,), (0,)), ((), ())),
-        preferred_element_type=jnp.float32,
-    )
-    up_term = lax.dot_general(
-        row_block,
-        lax.all_gather(up_grad, "tm", axis=0, tiled=True),
-        (((0,), (0,)), ((), ())),
-        preferred_element_type=jnp.float32,
-    )
-    return (losses, gate_term.astype(jnp.bfloat16), up_term.astype(jnp.bfloat16), grad_down)
+    cotangent = (row_coef[:, None] * probe.astype(jnp.float32)).astype(jnp.bfloat16)
+    grads = (row_coef[:, None] * shared[:, hidden_cols:].astype(jnp.float32)).astype(jnp.bfloat16)
+
+    def over_rows(left, right):
+        return lax.dot_general(
+            left, right, (((0,), (0,)), ((), ())), preferred_element_type=jnp.float32
+        ).astype(jnp.bfloat16)
+
+    return (
+        losses,
+        over_rows(all_rows, grads[:, :hidden_cols]),
+        over_rows(all_rows, grads[:, hidden_cols:]),
+        over_rows(hidden_all, cotangent),
+    )
 
 
 def solution(mesh):

time: 651 us -> 528 us (0.81)
  blocking collectives: 156 us -> 39.6 us
  waiting for transfers between devices: 335 us -> 316 us
  local copies, waits for them, and re-layouts: 29.4 us -> 41.3 us
  matrix products: 80 us -> 71.5 us
    all_gather x5 -> x0, blocking collectives: 112 us -> none  [the longest x1 36.1 us: body(): lax.all_gather(temporal_output_weight, 'dp', axis=1, tiled=True)]
    psum x1 -> x0, waiting for transfers between devices: 36.2 us -> none  [body(): lax.psum(vis_part.astype(jnp.bfloat16), 'tensor').astype(jnp.float32)]
    unnamed x10, waiting for transfers between devices: 31.2 us -> 0.67 us
    reduce_scatter x1 -> x3, waiting for transfers between devices: 11 us -> 41.5 us  [the longest x1 25 us: body(): lax.psum_scatter(vis_part.astype(jnp.bfloat16), 'tensor', scatter_dimensi...]
    transpose x0 -> x4, local copies, waits for them, and re-layouts: none -> 20.9 us  [gathered(): whole[:, :3].transpose(1, 0, 2, 3).reshape(3, n * rows, cols)]
    psum x1 -> x3, blocking collectives: 39.4 us -> 23.7 us  [body(): margin = lax.optimization_barrier(lax.psum(margin, axis))]
    all_gather x3 -> x4, waiting for transfers between devices: 178 us -> 191 us  [the longest x2 122 us: gathered(): lax.all_gather(jnp.concatenate([qkv, out[None]], axis=0), 'dp', axis=0)]
    reshape x0 -> x4, local copies, waits for them, and re-layouts: none -> 11.1 us  [the longest x2 9.59 us: gathered(): whole[:, :3].transpose(1, 0, 2, 3).reshape(3, n * rows, cols)]
  transfers between devices with their start and end apart: 10 -> 10, of which waited for: 9 -> 10; matrix products, arithmetic and copies ran while one was open for 6% -> 9% of each run, Pallas kernels for 0% -> 0%
where the time goes in v1:
time: 528 us; the launch traced here: 519 us
  waiting for transfers between devices  316 us (60%)
  matrix products  71.5 us (14%)
  local copies, waits for them, and re-layouts  41.3 us (8%)
  blocking collectives  39.6 us (8%)
  other arithmetic  27.5 us (5%)
  between operations  14.8 us (3%)
  starting transfers between devices  8.51 us (2%)
    all_gather x2, waiting for transfers between devices, gathered(): lax.all_gather(jnp.concatenate([qkv, out[None]], axis=0), 'dp', axis=0)  122 us
    all_gather x1, waiting for transfers between devices, body(): all_rows = lax.all_gather(normed_rows, ('dp', 'tensor'), axis=0, tiled=True)  50.7 us
    psum x1, waiting for transfers between devices, body(): lax.psum(partial_out.astype(jnp.bfloat16), 'tensor').astype(jnp.float32)  29.3 us
    reduce_scatter x1, waiting for transfers between devices, body(): lax.psum_scatter(jnp.concatenate([jnp.dot(row_block, w_gate, preferred_el...  29 us
    reduce_scatter x1, waiting for transfers between devices, body(): lax.psum_scatter(vis_part.astype(jnp.bfloat16), 'tensor', scatter_dimensi...  25 us
    psum x1, waiting for transfers between devices, body(): chosen_tokens = lax.psum(picked.astype(jnp.bfloat16), 'tm')  24.7 us
    psum x3, blocking collectives, body(): margin = lax.optimization_barrier(lax.psum(margin, axis))  23.7 us
    dot_general x3, matrix products, over_rows(): lax.dot_general(left, right, (((0,), (0,)), ((), ())), preferred_element_...  22.9 us
  transfers between devices with their start and end apart: 10, of which 10 were waited for; matrix products, arithmetic and copies ran while one was open for 9% of the time, Pallas kernels for 0%

profile of v1, /device:TPU:0, one launch (start us, length us, event | category | flops | bytes accessed | tf_op | source)
XLA Modules:
  0.0 519.3 jit_solution(15205512801139296623)
XLA Ops:
  10.2 9.7 %convolution_convert_fusion.9 = bf16[512,960]{0,1:T(8,128)(2,1)} fusion(bf16[512,4096]{1,0:T(8,128)(2,1)} %param.27, bf16[960,4096]{1,0:T(8,128)(2,1)} %param.26), kind=kOutput, calls=%fused_computation.29 | convolution fusion | flops 4027023360 | bytes 13041664 | tf_op jit(solution)/shard_map/dot_general | solution.py:70
  20.0 69.4 %all-gather.11.cloned.1.call-done = bf16[16,320,320]{2,1,0:T(8,128)(2,1)} async-done(((bf16[4,320,320]{2,1,0:T(8,128)(2,1)}), bf16[16,320,320]{2,1,0:T(8,128)(2,1)}) %all-gather.11.cloned.1.call-update) | async-done | bytes 3276816 | tf_op jit(solution)/shard_map/all_gather | solution.py:75
  93.1 6.2 %copy.53 = bf16[3,4,320,320]{2,1,3,0:T(4,128)(2,1)S(1)} copy(bf16[3,4,320,320]{3,2,0,1:T(8,128)(2,1)} %slice_bitcast_fusion.1) | data formatting | bytes 4915200 | tf_op jit(solution)/shard_map/transpose | solution.py:78
  114.6 29.3 %all-reduce.3.cloned.1.call-done = bf16[1,256,1280]{2,1,0:T(8,128)(2,1)} async-done(((bf16[1,256,1280]{2,1,0:T(8,128)(2,1)}), bf16[1,256,1280]{2,1,0:T(8,128)(2,1)}) %all-reduce.3.cloned.1.call-update) | async-done | bytes 655376 | tf_op jit(solution)/shard_map/psum | solution.py:102
  151.5 11.0 %all_to_all.12 = bf16[2,2,81920]{2,1,0:T(2,128)(2,1)S(1)} all-to-all(bf16[2,2,81920]{2,1,0:T(2,128)(2,1)S(1)} %reshape.131), channel_id=1, replica_groups=mesh['tm'=2,'tensor'=4,'dp'=4] {'tm'}, dimensions={0} | all-to-all | bytes 1310720 | tf_op jit(solution)/shard_map/all_to_all | solution.py:104
  169.4 53.1 %all-gather.13.cloned.1.call-done = bf16[16,320,320]{2,1,0:T(8,128)(2,1)} async-done(((bf16[4,320,320]{2,1,0:T(8,128)(2,1)}), bf16[16,320,320]{2,1,0:T(8,128)(2,1)}) %all-gather.13.cloned.1.call-update) | async-done | bytes 3276816 | tf_op jit(solution)/shard_map/all_gather | solution.py:75
  227.5 7.2 %copy.59 = bf16[3,4,320,320]{2,1,3,0:T(4,128)(2,1)} copy(bf16[3,4,320,320]{3,2,0,1:T(8,128)(2,1)} %slice_bitcast_fusion) | data formatting | bytes 4915200 | tf_op jit(solution)/shard_map/transpose | solution.py:78
  234.8 5.9 %reshape.113 = bf16[3,1280,320]{1,2,0:T(8,128)(2,1)} reshape(bf16[3,4,320,320]{2,1,3,0:T(4,128)(2,1)} %copy.59) | data formatting | bytes 4915200 | tf_op jit(solution)/shard_map/reshape | solution.py:78
  254.7 7.9 %all-reduce.5.cloned.1.call-start = ((), (), s32[]{:S(2)}) async-start(), calls=%async_computation.8 | async-start | bytes 655360 | tf_op jit(solution)/shard_map/psum | solution.py:132
  263.0 14.3 %reduce-scatter.7.cloned.1.call-done = bf16[2,128,320]{1,2,0:T(8,128)(2,1)} async-done(((bf16[2,128,1280]{1,2,0:T(8,128)(2,1)}), bf16[2,128,320]{1,2,0:T(8,128)(2,1)}) %reduce-scatter.7.cloned.1.call-update) | async-done | bytes 163856 | tf_op jit(solution)/shard_map/reduce_scatter | solution.py:114
  279.8 24.7 %all-reduce.5.cloned.1.call-done = bf16[128,1280]{1,0:T(8,128)(2,1)} async-done(((bf16[128,1280]{1,0:T(8,128)(2,1)}), bf16[128,1280]{1,0:T(8,128)(2,1)}) %all-reduce.5.cloned.1.call-update) | async-done | bytes 327696 | tf_op jit(solution)/shard_map/psum | solution.py:132
  304.4 6.7 %convolution_convert_fusion.3 = bf16[128,4096]{1,0:T(8,128)(2,1)} fusion(bf16[128,1280]{1,0:T(8,128)(2,1)} %all-reduce.5.cloned.1.call-done, bf16[1280,4096]{1,0:T(8,128)(2,1)} %bitcast.129), kind=kOutput, calls=%fused_computation.6 | convolution fusion | flops 1342701568 | bytes 11862016 | tf_op jit(solution)/shard_map/dot_general | solution.py:133
  311.2 25.0 %reduce-scatter.9.cloned.1.call-done = bf16[32,4096]{1,0:T(8,128)(2,1)} async-done(((bf16[128,4096]{1,0:T(8,128)(2,1)}), bf16[32,4096]{1,0:T(8,128)(2,1)}) %reduce-scatter.9.cloned.1.call-update) | async-done | bytes 262160 | tf_op jit(solution)/shard_map/reduce_scatter | solution.py:138
  344.1 50.7 %all-gather.7.cloned.1.call-done = bf16[512,4096]{1,0:T(8,128)(2,1)} async-done(((bf16[32,4096]{1,0:T(8,128)(2,1)}), bf16[512,4096]{1,0:T(8,128)(2,1)}) %all-gather.7.cloned.1.call-update) | async-done | bytes 4194320 | tf_op jit(solution)/shard_map/all_gather | solution.py:148
  394.8 8.9 %convolution_convert_fusion.7 = bf16[512,960]{0,1:T(8,128)(2,1)S(1)} fusion(bf16[512,4096]{1,0:T(8,128)(2,1)} %all-gather.7.cloned.1.call-done, bf16[4096,960]{0,1:T(8,128)(2,1)} %param.25), kind=kOutput, calls=%fused_computation.27 | convolution fusion | flops 4027023360 | bytes 13041664 | tf_op jit(solution)/shard_map/dot_general | solution.py:155
  403.7 6.9 %convolution_convert_fusion.8 = bf16[512,960]{0,1:T(8,128)(2,1)S(1)} fusion(bf16[512,4096]{1,0:T(8,128)(2,1)S(1)} %copy-done.10, bf16[4096,960]{0,1:T(8,128)(2,1)} %param.24), kind=kOutput, calls=%fused_computation.28 | convolution fusion | flops 4027023360 | bytes 13041664 | tf_op jit(solution)/shard_map/dot_general | solution.py:154
  412.1 29.0 %reduce-scatter.11.cloned.1.call-done = bf16[256,1920]{0,1:T(8,128)(2,1)} async-done(((bf16[512,1920]{0,1:T(8,128)(2,1)}), bf16[256,1920]{0,1:T(8,128)(2,1)}) %reduce-scatter.11.cloned.1.call-update) | async-done | bytes 983056 | tf_op jit(solution)/shard_map/reduce_scatter | solution.py:151
  444.9 6.9 %psum.45 = f32[16]{0:T(128)S(1)} all-reduce(f32[16]{0:T(128)S(1)} %convolution_bitcast_fusion), channel_id=1, replica_groups=mesh['tm'=2,'tensor'=4,'dp'=4] {'tensor'}, use_global_device_ids=true, to_apply=%region_17.18 | all-reduce | flops 16 | bytes 128 | tf_op jit(solution)/shard_map/psum | solution.py:187
  451.7 11.7 %psum.46 = f32[16]{0:T(128)S(1)} all-reduce(f32[16]{0:T(128)S(1)} %psum.45), channel_id=1, replica_groups=mesh['tm'=2,'tensor'=4,'dp'=4] {'dp'}, use_global_device_ids=true, to_apply=%region_18.19 | all-reduce | flops 16 | bytes 128 | tf_op jit(solution)/shard_map/psum | solution.py:187
  463.4 5.2 psum.47
  469.4 17.9 %all-gather.9.cloned.1.call-done = bf16[512,2880]{0,1:T(8,128)(2,1)} async-done(((bf16[256,2880]{0,1:T(8,128)(2,1)}), bf16[512,2880]{0,1:T(8,128)(2,1)}) %all-gather.9.cloned.1.call-update) | async-done | bytes 2949136 | tf_op jit(solution)/shard_map/all_gather | solution.py:188
  489.3 8.7 %convolution_convert_fusion.1 = bf16[4096,960]{0,1:T(8,128)(2,1)} fusion(bf16[512,4096]{1,0:T(8,128)(2,1)} %all-gather.7.cloned.1.call-done, bf16[512,1920]{0,1:T(8,128)(2,1)S(1)} %multiply_convert_fusion.2), kind=kOutput, calls=%fused_computation.4 | convolution fusion | flops 4030464000 | bytes 13041664 | tf_op jit(solution)/shard_map/dot_general | solution.py:200
  498.0 6.4 %convolution_convert_fusion = bf16[4096,960]{0,1:T(8,128)(2,1)} fusion(bf16[512,4096]{1,0:T(8,128)(2,1)S(1)} %copy-done.11, bf16[512,1920]{0,1:T(8,128)(2,1)S(1)} %multiply_convert_fusion.2), kind=kOutput, calls=%fused_computation.3 | convolution fusion | flops 4030464000 | bytes 13041664 | tf_op jit(solution)/shard_map/dot_general | solution.py:200
  504.4 7.8 %convolution_convert_fusion.2 = bf16[960,4096]{1,0:T(8,128)(2,1)} fusion(bf16[512,4096]{1,0:T(8,128)(2,1)S(1)} %copy-done.9, f32[512]{0:T(512)S(1)} %convert_multiply_fusion.3, bf16[512,2880]{0,1:T(8,128)(2,1)} %all-gather.9.cloned.1.call-done), kind=kOutput, calls=%fused_computation.5 | convolution fusion | flops 4036755456 | bytes 13043712 | tf_op jit(solution)/shard_map/dot_general | solution.py:200
  (113 shorter events, 74.2 us)
Async XLA Ops:
  7.2 2.5 copy-start
  7.2 82.2 %all-gather.11.cloned.1.call-start = ((), (), s32[]{:S(2)}) async-start(), calls=%async_computation.13 | async-start | bytes 4915200 | tf_op jit(solution)/shard_map/all_gather | solution.py:75
  9.7 134.2 %all-reduce.3.cloned.1.call-start = ((), (), s32[]{:S(2)}) async-start(), calls=%async_computation.5 | async-start | bytes 1310720 | tf_op jit(solution)/shard_map/psum | solution.py:102
  109.5 1.9 copy-start.4
  110.0 33.9 %copy-start.1 = (bf16[1,1,256,1280]{3,2,1,0:T(8,128)(2,1)S(1)}, bf16[1,1,256,1280]{3,2,1,0:T(8,128)(2,1)}, u32[]{:S(2)}) copy-start(bf16[1,1,256,1280]{3,2,1,0:T(8,128)(2,1)} %param.16) | copy-start | bytes 1966084
  111.3 111.1 %all-gather.13.cloned.1.call-start = ((), (), s32[]{:S(2)}) async-start(), calls=%async_computation.14 | async-start | bytes 4915200 | tf_op jit(solution)/shard_map/all_gather | solution.py:75
  113.7 129.1 %reduce-scatter.5.cloned.1.call-start = ((), (), s32[]{:S(2)}) async-start(), calls=%async_computation.6 | async-start | bytes 1474560 | tf_op jit(solution)/shard_map/reduce_scatter | solution.py:87
  114.2 163.1 %reduce-scatter.7.cloned.1.call-start = ((), (), s32[]{:S(2)}) async-start(), calls=%async_computation.7 | async-start | bytes 819200 | tf_op jit(solution)/shard_map/reduce_scatter | solution.py:114
  253.1 9.5 %copy-start.8 = (s32[128]{0:T(128)S(1)}, s32[128]{0:T(128)}, u32[]{:S(2)}) copy-start(s32[128]{0:T(128)} %param.31) | copy-start | bytes 1540
  254.7 49.8 %all-reduce.5.cloned.1.call-start = ((), (), s32[]{:S(2)}) async-start(), calls=%async_computation.8 | async-start | bytes 655360 | tf_op jit(solution)/shard_map/psum | solution.py:132
  279.7 56.5 %reduce-scatter.9.cloned.1.call-start = ((), (), s32[]{:S(2)}) async-start(), calls=%async_computation.9 | async-start | bytes 1310720 | tf_op jit(solution)/shard_map/reduce_scatter | solution.py:138
  304.4 31.8 %copy-start.3 = (bf16[128,4096]{1,0:T(8,128)(2,1)S(1)}, bf16[128,4096]{1,0:T(8,128)(2,1)}, u32[]{:S(2)}) copy-start(bf16[128,4096]{1,0:T(8,128)(2,1)} %param.22) | copy-start | bytes 3145732
  304.4 37.8 %copy-start.5 = (f32[4096]{0:T(1024)S(1)}, f32[4096]{0:T(1024)}, u32[]{:S(2)}) copy-start(f32[4096]{0:T(1024)} %param.23) | copy-start | bytes 49156
  311.1 83.7 %all-gather.7.cloned.1.call-start = ((), (), s32[]{:S(2)}) async-start(), calls=%async_computation.10 | async-start | bytes 4456448 | tf_op jit(solution)/shard_map/all_gather | solution.py:148
  344.1 97.0 %reduce-scatter.11.cloned.1.call-start = ((), (), s32[]{:S(2)}) async-start(), calls=%async_computation.11 | async-start | bytes 2949120 | tf_op jit(solution)/shard_map/reduce_scatter | solution.py:151
  394.8 8.9 %copy-start.10 = (bf16[512,4096]{1,0:T(8,128)(2,1)S(1)}, bf16[512,4096]{1,0:T(8,128)(2,1)}, u32[]{:S(2)}) copy-start(bf16[512,4096]{1,0:T(8,128)(2,1)} %all-gather.7.cloned.1.call-done) | copy-start | bytes 12582916
  412.1 30.4 %copy-start.2 = (bf16[256,960]{0,1:T(8,128)(2,1)S(1)}, bf16[256,960]{0,1:T(8,128)(2,1)}, u32[]{:S(2)}) copy-start(bf16[256,960]{0,1:T(8,128)(2,1)} %reduce-scatter.5.cloned.1.call-done) | copy-start | bytes 1474564
  412.1 75.3 %all-gather.9.cloned.1.call-start = ((), (), s32[]{:S(2)}) async-start(), calls=%async_computation.12 | async-start | bytes 4423680 | tf_op jit(solution)/shard_map/all_gather | solution.py:188
  443.2 1.3 copy-start.6
  443.2 1.3 copy-start.7
  443.2 25.4 %copy-start.12 = (f32[16]{0:T(128)S(1)}, f32[16]{0:T(128)}, u32[]{:S(2)}) copy-start(f32[16]{0:T(128)} %param.28) | copy-start | bytes 196
  489.3 8.7 %copy-start.11 = (bf16[512,4096]{1,0:T(8,128)(2,1)S(1)}, bf16[512,4096]{1,0:T(8,128)(2,1)}, u32[]{:S(2)}) copy-start(bf16[512,4096]{1,0:T(8,128)(2,1)} %all-gather.7.cloned.1.call-done) | copy-start | bytes 12582916
  498.0 6.4 %copy-start.9 = (bf16[512,4096]{1,0:T(8,128)(2,1)S(1)}, bf16[512,4096]{1,0:T(8,128)(2,1)}, u32[]{:S(2)}) copy-start(bf16[512,4096]{1,0:T(8,128)(2,1)} %param.27) | copy-start | bytes 12582916
Sparse Core Ops, SparseCore 0:
  10.2 79.1 all-gather.10
  111.5 32.3 all-reduce.2
  146.0 76.4 all-gather.12
  224.6 18.1 reduce-scatter.4
  254.8 22.4 reduce-scatter.6
  280.1 24.2 all-reduce.4
  311.3 24.8 reduce-scatter.8
  344.2 50.5 all-gather.6
  412.2 28.8 reduce-scatter.10
  444.6 42.7 all-gather.8
